TPU v7x, 32 devices: a whole 2x2x4 slice. The times are simulated.
32 devices in a mesh: dp: 2 (over x), fsdp: 16 (over z, y, core).
Axes of the slice: x: 2, y: 2, z: 4, core: 2. Of those that a mesh axis runs over, the one named last changes fastest.
Arguments:
- hidden: bfloat16 [64, 64, 768], P(('dp', 'fsdp')), may hold values from -6 to 6
- lengths: int32 [64], P(('dp', 'fsdp')), may hold values from 5 to 32, as said below
- features: bfloat16 [64, 257, 1408], P(('dp', 'fsdp')), may hold values from -6 to 6
- cotangent: bfloat16 [64, 64, 768], P(('dp', 'fsdp')), may hold values from -6 to 6
- self_params: bfloat16 [2363392], P('fsdp')
- cross_params: bfloat16 [3346432], P('fsdp')
- ffn_params: bfloat16 [9449472], P('fsdp')
Outputs:
- mixed: bfloat16 [64, 64, 768], P(('dp', 'fsdp'))
- hidden_grad: bfloat16 [64, 64, 768], P(('dp', 'fsdp'))
- self_grad: float32 [2363392], P('fsdp')
- cross_grad: float32 [3346432], P('fsdp')
- ffn_grad: float32 [9449472], P('fsdp')
Inputs may be any that keep to these rules, and one draw needn't show every extreme that they name: lengths lie between 5 and 32; some item of every draw has 32.
All inputs are finite; a program needn't handle non-finite values.
Results may differ from a plain program's by a relative error of at most 0.017.
Values may be sent and summed in bfloat16 or wider, within the bound.
A program may use at most 384 MiB of HBM per device.

v0:
```python
from functools import partial
import math
import jax
import jax.numpy as jnp
from jax import lax
from jax.sharding import PartitionSpec as P

D = 768
HEADS = 12
HDIM = 64
F = 3072
E = 1408
NQ = 32
EPS = 1e-06
SCALE = 0.125


def self_layout():
    return [(D, D)] * 4 + [(D,)] * 5


def cross_layout():
    return [(D, D), (E, D), (E, D), (D, D)] + [(D,)] * 5


def ffn_layout():
    return [(D, F), (F,), (F, D), (D,), (D,), (D,)] * 2


def split_flat(flat_vec, layouts):
    pieces = []
    offset = 0
    for layout in layouts:
        amount = math.prod(layout)
        pieces.append(flat_vec[offset : offset + amount].reshape(layout))
        offset = offset + amount
    return pieces


def join_flat(pieces, length):
    flat_vec = jnp.concatenate([piece.reshape(-1) for piece in pieces])
    return jnp.pad(flat_vec, (0, length - flat_vec.shape[0]))


def regroup(flat_vec):
    groups = lax.axis_size("fsdp")
    replicas = lax.axis_size("dp")
    return flat_vec.reshape(groups, replicas, -1).transpose(1, 0, 2).reshape(-1)


def matmul(left, right):
    return jnp.dot(left, right, preferred_element_type=jnp.float32)


def matmul_left(left, right):
    return lax.dot_general(
        left, right, (((0,), (0,)), ((), ())), preferred_element_type=jnp.float32
    )


def matmul_right(left, right):
    return lax.dot_general(
        left, right, (((1,), (1,)), ((), ())), preferred_element_type=jnp.float32
    )


def column_sum(values):
    return jnp.sum(values.astype(jnp.float32), 0)


def layer_norm(values, gain, shift):
    average = jnp.mean(values, -1, keepdims=True)
    centered = values - average
    variance = jnp.mean(centered * centered, -1, keepdims=True)
    return centered * lax.rsqrt(variance + EPS) * gain + shift


def norm_backward(summed, gain, shift, grad_out):
    _, norm_pull = jax.vjp(layer_norm, summed, gain.astype(jnp.float32), shift.astype(jnp.float32))
    return norm_pull(grad_out)


def heads(rows, items):
    return rows.reshape(items, -1, HEADS, HDIM)


def score_block(query, keys, mask):
    scores = jnp.einsum("iqhd,ikhd->ihqk", query, keys, preferred_element_type=jnp.float32) * SCALE
    if mask is not None:
        scores = jnp.where(mask, scores, -1e30)
    return scores


def attend(query, keys, values, mask):
    scores = score_block(query, keys, mask)
    top_sum = jax.nn.logsumexp(scores, axis=-1)
    probs = jnp.exp(scores - top_sum[..., None]).astype(jnp.bfloat16)
    context = jnp.einsum("ihqk,ikhd->iqhd", probs, values, preferred_element_type=jnp.float32)
    return (context, top_sum)


def attend_back(query, keys, values, mask, top_sum, grad_context):
    probs = jnp.exp(score_block(query, keys, mask) - top_sum[..., None])
    grad_probs = jnp.einsum(
        "iqhd,ikhd->ihqk", grad_context, values, preferred_element_type=jnp.float32
    )
    inner = jnp.sum(probs * grad_probs, -1, keepdims=True)
    grad_scores = (probs * (grad_probs - inner)).astype(jnp.bfloat16)
    grad_query = (
        jnp.einsum("ihqk,ikhd->iqhd", grad_scores, keys, preferred_element_type=jnp.float32) * SCALE
    )
    grad_keys = (
        jnp.einsum("ihqk,iqhd->ikhd", grad_scores, query, preferred_element_type=jnp.float32)
        * SCALE
    )
    grad_values = jnp.einsum(
        "ihqk,iqhd->ikhd",
        probs.astype(jnp.bfloat16),
        grad_context,
        preferred_element_type=jnp.float32,
    )
    return (grad_query, grad_keys, grad_values)


def linear_back(inputs, weight, grad_out):
    return (matmul_left(inputs, grad_out), column_sum(grad_out), matmul_right(grad_out, weight))


def ffn_forward(rows, params):
    w_in, b_in, w_out, b_out, gain, shift = params
    rows_low = rows.astype(jnp.bfloat16)
    hidden_pre = matmul(rows_low, w_in) + b_in
    activated = jax.nn.gelu(hidden_pre, approximate=True).astype(jnp.bfloat16)
    summed = rows + (matmul(activated, w_out) + b_out)
    final = layer_norm(summed, gain.astype(jnp.float32), shift.astype(jnp.float32))
    return (final, (rows_low, hidden_pre, activated, summed))


def ffn_backward(grad_out, kept, params):
    w_in, b_in, w_out, b_out, gain, shift = params
    rows_low, hidden_pre, activated, summed = kept
    grad_sum, grad_gain, grad_shift = norm_backward(summed, gain, shift, grad_out)
    grad_branch = grad_sum.astype(jnp.bfloat16)
    grad_w_out, grad_b_out, grad_act = linear_back(activated, w_out, grad_branch)
    _, gelu_pull = jax.vjp(partial(jax.nn.gelu, approximate=True), hidden_pre)
    grad_pre = gelu_pull(grad_act)[0].astype(jnp.bfloat16)
    grad_w_in, grad_b_in, grad_rows = linear_back(rows_low, w_in, grad_pre)
    return (
        grad_sum + grad_rows,
        [grad_w_in, grad_b_in, grad_w_out, grad_b_out, grad_gain, grad_shift],
    )


def per_device(hidden, lengths, features, cotangent, self_params, cross_params, ffn_params):
    items, seq, width = hidden.shape
    self_full = lax.all_gather(self_params, "fsdp", axis=0, tiled=True)
    self_parts = split_flat(self_full, self_layout())
    w_q, w_k, w_v, w_o, b_q, b_v, b_o, gain_one, shift_one = self_parts
    positions = jnp.arange(seq)
    rows_at = positions[:, None]
    cols_at = positions[None, :]
    allowed = (cols_at < NQ)[None] | ((rows_at >= NQ) & (cols_at <= rows_at))[None] & (
        cols_at[None] < NQ + lengths[:, None, None]
    )
    allowed = allowed[:, None]
    inputs = hidden.reshape(-1, width)
    query_low = (matmul(inputs, w_q) + b_q).astype(jnp.bfloat16)
    key_low = matmul(inputs, w_k).astype(jnp.bfloat16)
    value_low = (matmul(inputs, w_v) + b_v).astype(jnp.bfloat16)
    context, self_top = attend(
        heads(query_low, items), heads(key_low, items), heads(value_low, items), allowed
    )
    context_low = context.reshape(-1, width).astype(jnp.bfloat16)
    summed_one = inputs.astype(jnp.float32) + (matmul(context_low, w_o) + b_o)
    first = layer_norm(summed_one, gain_one.astype(jnp.float32), shift_one.astype(jnp.float32))
    first_items = first.reshape(items, seq, width)
    query_rows = first_items[:, :NQ].reshape(-1, width)
    text_rows = first_items[:, NQ:].reshape(-1, width)
    cross_full = lax.all_gather(cross_params, "fsdp", axis=0, tiled=True)
    cross_parts = split_flat(cross_full, cross_layout())
    cross_wq, cross_wk, cross_wv, cross_wo, cross_bq, cross_bv, cross_bo, gain_two, shift_two = (
        cross_parts
    )
    query_in = query_rows.astype(jnp.bfloat16)
    image_rows = features.reshape(-1, features.shape[-1])
    cross_query = (matmul(query_in, cross_wq) + cross_bq).astype(jnp.bfloat16)
    cross_key = matmul(image_rows, cross_wk).astype(jnp.bfloat16)
    cross_value = (matmul(image_rows, cross_wv) + cross_bv).astype(jnp.bfloat16)
    cross_context, cross_top = attend(
        heads(cross_query, items), heads(cross_key, items), heads(cross_value, items), None
    )
    cross_low = cross_context.reshape(-1, width).astype(jnp.bfloat16)
    summed_two = query_rows + (matmul(cross_low, cross_wo) + cross_bo)
    second = layer_norm(summed_two, gain_two.astype(jnp.float32), shift_two.astype(jnp.float32))
    ffn_full = lax.all_gather(ffn_params, "fsdp", axis=0, tiled=True)
    ffn_parts = split_flat(ffn_full, ffn_layout())
    query_final, query_kept = ffn_forward(second, ffn_parts[:6])
    text_final, text_kept = ffn_forward(text_rows, ffn_parts[6:])
    mixed = jnp.concatenate(
        [query_final.reshape(items, NQ, width), text_final.reshape(items, -1, width)], 1
    ).astype(jnp.bfloat16)
    grad_items = cotangent.astype(jnp.float32)
    grad_query_final = grad_items[:, :NQ].reshape(-1, width)
    grad_text_final = grad_items[:, NQ:].reshape(-1, width)
    ffn_back = split_flat(lax.all_gather(ffn_params, "fsdp", axis=0, tiled=True), ffn_layout())
    grad_second, query_grads = ffn_backward(grad_query_final, query_kept, ffn_back[:6])
    grad_text, text_grads = ffn_backward(grad_text_final, text_kept, ffn_back[6:])
    ffn_flat_grad = join_flat(query_grads + text_grads, ffn_full.shape[0])
    ffn_grad = lax.psum_scatter(
        regroup(ffn_flat_grad), ("dp", "fsdp"), scatter_dimension=0, tiled=True
    )
    cross_back = split_flat(
        lax.all_gather(cross_params, "fsdp", axis=0, tiled=True), cross_layout()
    )
    grad_summed_two, grad_gain_two, grad_shift_two = norm_backward(
        summed_two, cross_back[7], cross_back[8], grad_second
    )
    grad_cross_out = grad_summed_two.astype(jnp.bfloat16)
    grad_cross_wo, grad_cross_bo, grad_cross_ctx = linear_back(
        cross_low, cross_back[3], grad_cross_out
    )
    grad_cq, grad_ck, grad_cv = attend_back(
        heads(cross_query, items),
        heads(cross_key, items),
        heads(cross_value, items),
        None,
        cross_top,
        heads(grad_cross_ctx.astype(jnp.bfloat16), items),
    )
    grad_cq = grad_cq.reshape(-1, width).astype(jnp.bfloat16)
    grad_ck = grad_ck.reshape(-1, width).astype(jnp.bfloat16)
    grad_cv = grad_cv.reshape(-1, width).astype(jnp.bfloat16)
    grad_cross_wq, grad_cross_bq, grad_query_in = linear_back(query_in, cross_back[0], grad_cq)
    grad_cross_wk = matmul_left(image_rows, grad_ck)
    grad_cross_wv = matmul_left(image_rows, grad_cv)
    grad_cross_bv = column_sum(grad_cv)
    grad_query_rows = grad_summed_two + grad_query_in
    cross_list = [
        grad_cross_wq,
        grad_cross_wk,
        grad_cross_wv,
        grad_cross_wo,
        grad_cross_bq,
        grad_cross_bv,
        grad_cross_bo,
        grad_gain_two,
        grad_shift_two,
    ]
    cross_flat_grad = join_flat(cross_list, cross_full.shape[0])
    cross_grad = lax.psum_scatter(
        regroup(cross_flat_grad), ("dp", "fsdp"), scatter_dimension=0, tiled=True
    )
    self_back = split_flat(lax.all_gather(self_params, "fsdp", axis=0, tiled=True), self_layout())
    grad_first = jnp.concatenate(
        [grad_query_rows.reshape(items, NQ, width), grad_text.reshape(items, -1, width)], 1
    ).reshape(-1, width)
    grad_summed_one, grad_gain_one, grad_shift_one = norm_backward(
        summed_one, self_back[7], self_back[8], grad_first
    )
    grad_attn = grad_summed_one.astype(jnp.bfloat16)
    grad_w_o, grad_b_o, grad_ctx = linear_back(context_low, self_back[3], grad_attn)
    grad_q, grad_k, grad_v = attend_back(
        heads(query_low, items),
        heads(key_low, items),
        heads(value_low, items),
        allowed,
        self_top,
        heads(grad_ctx.astype(jnp.bfloat16), items),
    )
    grad_q = grad_q.reshape(-1, width).astype(jnp.bfloat16)
    grad_k = grad_k.reshape(-1, width).astype(jnp.bfloat16)
    grad_v = grad_v.reshape(-1, width).astype(jnp.bfloat16)
    grad_w_q, grad_b_q, input_from_q = linear_back(inputs, self_back[0], grad_q)
    grad_w_k = matmul_left(inputs, grad_k)
    input_from_k = matmul_right(grad_k, self_back[1])
    grad_w_v, grad_b_v, input_from_v = linear_back(inputs, self_back[2], grad_v)
    hidden_grad = (
        (grad_summed_one + input_from_q + input_from_k + input_from_v)
        .reshape(items, seq, width)
        .astype(jnp.bfloat16)
    )
    self_list = [
        grad_w_q,
        grad_w_k,
        grad_w_v,
        grad_w_o,
        grad_b_q,
        grad_b_v,
        grad_b_o,
        grad_gain_one,
        grad_shift_one,
    ]
    self_flat_grad = join_flat(self_list, self_full.shape[0])
    self_grad = lax.psum_scatter(
        regroup(self_flat_grad), ("dp", "fsdp"), scatter_dimension=0, tiled=True
    )
    self_grad, cross_grad, ffn_grad = (
        lax.all_gather(self_grad.astype(jnp.bfloat16), "dp", axis=0, tiled=True).astype(
            self_grad.dtype
        ),
        lax.all_gather(cross_grad.astype(jnp.bfloat16), "dp", axis=0, tiled=True).astype(
            cross_grad.dtype
        ),
        lax.all_gather(ffn_grad.astype(jnp.bfloat16), "dp", axis=0, tiled=True).astype(
            ffn_grad.dtype
        ),
    )
    return (mixed, hidden_grad, self_grad, cross_grad, ffn_grad)


def solution(mesh):
    return jax.shard_map(
        per_device,
        mesh=mesh,
        in_specs=(
            P(("dp", "fsdp"), None, None),
            P(("dp", "fsdp")),
            P(("dp", "fsdp"), None, None),
            P(("dp", "fsdp"), None, None),
            P("fsdp"),
            P("fsdp"),
            P("fsdp"),
        ),
        out_specs=(
            P(("dp", "fsdp"), None, None),
            P(("dp", "fsdp"), None, None),
            P("fsdp"),
            P("fsdp"),
            P("fsdp"),
        ),
        check_vma=False,
    )
```

profile of v0, /device:TPU:0, one launch (start us, length us, event | category | flops | bytes accessed | tf_op | source)
XLA Modules:
  0.0 2604.6 jit_solution(10896527017699016095)
XLA Ops:
  17.5 14.2 reshape.500
  35.5 60.6 %all-gather.11.cloned.1.call-done = bf16[16,1,147712]{2,1,0:T(2,128)(2,1)} async-done(((bf16[1,1,147712]{2,1,0:T(2,128)(2,1)}), bf16[16,1,147712]{2,1,0:T(2,128)(2,1)}) %all-gather.11.cloned.1.call-update) | async-done | bytes 4726800 | tf_op jit(solution)/shard_map/all_gather | solution.py:156
  96.1 78.1 %reduce.11 = bf16[16,147712]{1,0:T(8,128)(2,1)} reduce(bf16[16,1,147712]{2,1,0:T(2,128)(2,1)} %all-gather.11.cloned.1.call-done, bf16[]{:T(256)} %constant.79), dimensions={1}, to_apply=%all-gather.reduce_sub_computation | reduce | bytes 9453570 | tf_op jit(solution)/shard_map/all_gather | solution.py:156
  174.2 10.1 reshape.497
  209.2 141.5 %reduce.12 = bf16[16,209152]{1,0:T(8,128)(2,1)} reduce(bf16[16,1,209152]{2,1,0:T(2,128)(2,1)} %all-gather.13.cloned.1.call-done, bf16[]{:T(256)} %constant.79), dimensions={1}, to_apply=%all-gather.1.reduce_sub_computation | reduce | bytes 13385730 | tf_op jit(solution)/shard_map/all_gather | solution.py:179
  350.8 14.0 reshape.499
  420.2 400.6 %reduce.13 = bf16[16,590592]{1,0:T(8,128)(2,1)} reduce(bf16[16,1,590592]{2,1,0:T(2,128)(2,1)} %all-gather.15.cloned.1.call-done, bf16[]{:T(256)} %constant.79), dimensions={1}, to_apply=%all-gather.2.reduce_sub_computation | reduce | bytes 37797888 | tf_op jit(solution)/shard_map/all_gather | solution.py:195
  820.8 43.1 %reshape.501 = bf16[9449472]{0:T(1024)(128)(2,1)} reshape(bf16[16,590592]{1,0:T(8,128)(2,1)} %reduce.13) | data formatting | bytes 37797888
  863.9 14.0 fusion.71
  880.7 8.2 slice.166
  888.9 9.2 slice.169
  913.7 9.3 slice.177
  1038.7 8.6 pad.12
  1047.3 10.3 reshape.482
  1138.5 10.0 pad.13
  1148.6 13.4 reshape.488
  1162.0 10.4 copy.156
  1172.4 9.8 reshape.489
  1192.0 10.8 reshape.491
  1210.0 10.8 reshape.493
  1221.4 8.3 constant_dynamic-update-slice_fusion.6
  1233.6 80.5 %dynamic-update-slice.6 = f32[9447936]{0:T(1024)} dynamic-update-slice(f32[9447936]{0:T(1024)} %constant_dynamic-update-slice_fusion.25, f32[2359296]{0:T(1024)} %bitcast.168, s32[]{} %constant.91) | dynamic-update-slice | bytes 18874372
  1315.4 80.5 %dynamic-update-slice.8 = f32[9447936]{0:T(1024)} dynamic-update-slice(f32[9447936]{0:T(1024)} %constant_dynamic-update-slice_fusion.24, f32[2359296]{0:T(1024)} %reshape.493, s32[]{} %constant.93) | dynamic-update-slice | bytes 18874372
  1399.8 27.1 %pad.14 = f32[9449472]{0:T(1024)} pad(f32[9447936]{0:T(1024)} %constant_dynamic-update-slice_fusion.21, f32[]{:T(128)} %constant.23.clone.1), padding=0_1536 | pad | bytes 75589632 | tf_op jit(solution)/shard_map/jit(_pad)/pad | solution.py:42
  1426.9 59.6 %reshape.494 = f32[16,2,295296]{2,1,0:T(2,128)} reshape(f32[9449472]{0:T(1024)} %pad.14) | data formatting | bytes 75595776 | tf_op jit(solution)/shard_map/reshape | solution.py:48
  1486.5 29.9 %copy.157 = f32[2,16,295296]{2,1,0:T(8,128)} copy(f32[2,16,295296]{2,0,1:T(2,128)} %bitcast.161) | data formatting | bytes 75595776 | tf_op jit(solution)/shard_map/transpose | solution.py:48
  1516.4 31.6 %reshape.495 = f32[9449472]{0:T(1024)} reshape(f32[2,16,295296]{2,1,0:T(8,128)} %copy.157) | data formatting | bytes 75595776 | tf_op jit(solution)/shard_map/reshape | solution.py:48
  1548.0 960.9 %all-reduce.8 = (bf16[2363392]{0:T(1024)(128)(2,1)}, bf16[3346432]{0:T(1024)(128)(2,1)}, bf16[9449472]{0:T(1024)(128)(2,1)}) all-reduce(f32[2363392]{0:T(1024)} %reshape.483, f32[3346432]{0:T(1024)} %reshape.489, f32[9449472]{0:T(1024)} %reshape.495), channel_id=2, replica_groups=mesh['dp'=2,'fsdp'=16] {'dp','fsdp'}, use_global_device_ids=true, to_apply=%region_28.29.clone | all-reduce | flops 15159296 | bytes 90955776
  2510.1 8.6 all-gather.3
  2531.3 14.9 all-gather.4
  2557.1 10.7 all-gather.17.cloned.1.call-done
  2567.8 26.9 %convert_reduce_fusion = f32[2,295296]{1,0:T(2,128)S(1)} fusion(bf16[2,1,295296]{2,1,0:T(2,128)(2,1)} %all-gather.17.cloned.1.call-done), kind=kLoop, calls=%fused_computation.6 | loop fusion | flops 590592 | bytes 3543552 | tf_op jit(solution)/shard_map/convert_element_type | solution.py:304
  (488 shorter events, 362.6 us)
Async XLA Ops:
  7.2 10.3 copy-start.56
  7.2 88.9 %all-gather.11.cloned.1.call-start = ((), (), s32[]{:S(2)}) async-start(), calls=%async_computation | async-start | bytes 10044416 | tf_op jit(solution)/shard_map/all_gather | solution.py:156
  11.7 197.5 %all-gather.13.cloned.1.call-start = ((), (), s32[]{:S(2)}) async-start(), calls=%async_computation.1 | async-start | bytes 14222336 | tf_op jit(solution)/shard_map/all_gather | solution.py:179
  17.4 14.4 copy-start.34
  17.4 402.8 %all-gather.15.cloned.1.call-start = ((), (), s32[]{:S(2)}) async-start(), calls=%async_computation.2 | async-start | bytes 40160256 | tf_op jit(solution)/shard_map/all_gather | solution.py:195
  31.7 2536.1 %all-gather.17.cloned.1.call-start = ((), (), s32[]{:S(2)}) async-start(), calls=%async_computation.3 | async-start | bytes 3543552 | tf_op jit(solution)/shard_map/all_gather | solution.py:304
  204.9 145.9 %copy-start.7 = (bf16[768,768]{1,0:T(8,128)(2,1)}, bf16[768,768]{1,0:T(8,128)(2,1)S(1)}, u32[]{:S(2)}) copy-start(bf16[768,768]{1,0:T(8,128)(2,1)S(1)} %reshape.456) | copy-start | bytes 3538948
  207.8 143.0 %copy-start.44 = (f32[2,32,768]{2,1,0:T(8,128)}, f32[2,32,768]{2,1,0:T(8,128)S(1)}, u32[]{:S(2)}) copy-start(f32[2,32,768]{2,1,0:T(8,128)S(1)} %get-tuple-element.72) | copy-start | bytes 589828
  208.6 196.8 %copy-start.59 = (bf16[2,32,768]{2,1,0:T(8,128)(2,1)}, bf16[2,32,768]{2,1,0:T(8,128)(2,1)S(1)}, u32[]{:S(2)}) copy-start(bf16[2,32,768]{2,1,0:T(8,128)(2,1)S(1)} %get-tuple-element.69) | copy-start | bytes 294916
  898.2 12.2 slice-start.2
  901.8 8.5 slice-start.3
  992.6 12.9 copy-start.40
  994.2 19.5 copy-start.46
  1031.3 6.8 copy-start.95
  1031.3 6.8 copy-start.96
  1131.2 6.8 copy-start.106
  1192.0 10.8 copy-start.51
  1192.0 10.8 copy-start.64
  1210.0 10.8 copy-start.113
  1221.4 8.3 copy-start.103
  1221.4 9.6 copy-start.102
  1221.4 11.0 copy-start.101
  1233.6 80.5 %copy-start.114 = (f32[3072]{0:T(1024)S(1)}, f32[3072]{0:T(1024)}, u32[]{:S(2)}) copy-start(f32[3072]{0:T(1024)} %get-tuple-element.21) | copy-start | bytes 36868
  1315.4 80.5 %copy-start.105 = (f32[768]{0:T(1024)S(1)}, f32[768]{0:T(1024)}, u32[]{:S(2)}) copy-start(f32[768]{0:T(1024)} %get-tuple-element.19) | copy-start | bytes 9220
  1315.4 81.8 %copy-start.104 = (f32[768]{0:T(1024)S(1)}, f32[768]{0:T(1024)}, u32[]{:S(2)}) copy-start(f32[768]{0:T(1024)} %get-tuple-element.7) | copy-start | bytes 9220
  1315.4 83.1 %copy-start.100 = (f32[768]{0:T(1024)S(1)}, f32[768]{0:T(1024)}, u32[]{:S(2)}) copy-start(f32[768]{0:T(1024)} %get-tuple-element.13) | copy-start | bytes 9220
  2546.2 8.5 copy-start.4
  2546.2 8.5 copy-start.30
  2546.2 8.5 copy-start.39
  2546.2 8.5 copy-start.122
  2547.5 6.5 copy-start.75
  2547.5 6.5 copy-start.76
  (107 other events, 326.7 us)
Sparse Core Ops, SparseCore 0:
  11.8 84.2 all-gather.10
  98.9 103.9 all-gather.12
  205.1 186.1 all-gather.14
  2531.4 36.2 all-gather.16
where the time goes:
time: 2630 us; the launch traced here: 2600 us
  blocking collectives  984 us (37%)
  local copies, waits for them, and re-layouts  767 us (29%)
  other arithmetic  672 us (26%)
  matrix products  94.1 us (4%)
  waiting for transfers between devices  71.3 us (3%)
    unnamed x1, blocking collectives  961 us
    all_gather x1, other arithmetic, per_device(): ffn_full = lax.all_gather(ffn_params, 'fsdp', axis=0, tiled=True)  401 us
    unnamed x312, local copies, waits for them, and re-layouts  337 us
    all_gather x1, other arithmetic, per_device(): cross_full = lax.all_gather(cross_params, 'fsdp', axis=0, tiled=True)  142 us
    reshape x6, local copies, waits for them, and re-layouts, regroup(): return flat_vec.reshape(groups, replicas, -1).transpose(1, 0, 2).reshape(-1)  133 us
    all_gather x1, other arithmetic, per_device(): self_full = lax.all_gather(self_params, 'fsdp', axis=0, tiled=True)  78.1 us
    all_gather x1, waiting for transfers between devices, per_device(): self_full = lax.all_gather(self_params, 'fsdp', axis=0, tiled=True)  60.6 us
  transfers between devices with their start and end apart: 4, of which 2 were waited for; matrix products, arithmetic and copies ran while one was open for 14% of the time, Pallas kernels for 0%

commit v1 on v0

--- a/solution.py
+++ b/solution.py
@@ -153,7 +153,23 @@
 
 def per_device(hidden, lengths, features, cotangent, self_params, cross_params, ffn_params):
     items, seq, width = hidden.shape
-    self_full = lax.all_gather(self_params, "fsdp", axis=0, tiled=True)
+    ways, here, turn = (lax.axis_size("fsdp"), lax.axis_index("fsdp"), self_params.shape[0])
+    shape = [n * ways if d == 0 else n for d, n in enumerate(self_params.shape)]
+    full = lax.dynamic_update_slice_in_dim(
+        jnp.zeros(shape, self_params.dtype), self_params, here * turn, axis=0
+    )
+    going_up = going_down = self_params
+    for far in range(1, ways // 2 + 1):
+        going_up = lax.ppermute(going_up, "fsdp", [(d, (d + 1) % ways) for d in range(ways)])
+        full = lax.dynamic_update_slice_in_dim(full, going_up, (here - far) % ways * turn, axis=0)
+        if 2 * far < ways:
+            going_down = lax.ppermute(
+                going_down, "fsdp", [(d, (d - 1) % ways) for d in range(ways)]
+            )
+            full = lax.dynamic_update_slice_in_dim(
+                full, going_down, (here + far) % ways * turn, axis=0
+            )
+    self_full = full
     self_parts = split_flat(self_full, self_layout())
     w_q, w_k, w_v, w_o, b_q, b_v, b_o, gain_one, shift_one = self_parts
     positions = jnp.arange(seq)

time: 2630 us -> 2780 us (1.057)
  local copies, waits for them, and re-layouts: 767 us -> 882 us
  starting transfers between devices: 0.16 us -> 33.9 us
    dynamic_update_slice x0 -> x16, local copies, waits for them, and re-layouts: none -> 93.8 us  [the longest x8 46.9 us: per_device(): lax.dynamic_update_slice_in_dim(full, going_up, (here - far) % ways * tur...]
    all_gather x1, waiting for transfers between devices: 60.6 us -> 0.01 us  [per_device(): lax.all_gather(self_params, 'fsdp', axis=0, tiled=True)]
    ppermute x0 -> x15, waiting for transfers between devices: none -> 49 us  [the longest x7 37.1 us: per_device(): lax.ppermute(going_down, 'fsdp', [(d, (d - 1) % ways) for d in range(ways)])]
    ppermute x0 -> x15, starting transfers between devices: none -> 33.7 us  [the longest x7 32.6 us: per_device(): lax.ppermute(going_down, 'fsdp', [(d, (d - 1) % ways) for d in range(ways)])]
    unnamed x312 -> x304, local copies, waits for them, and re-layouts: 337 us -> 333 us
    slice x7 -> x8, local copies, waits for them, and re-layouts: 52.2 us -> 56 us  [split_flat(): pieces.append(flat_vec[offset:offset + amount].reshape(layout))]
  transfers between devices with their start and end apart: 4 -> 19, of which waited for: 2 -> 11; matrix products, arithmetic and copies ran while one was open for 14% -> 17% of each run, Pallas kernels for 0% -> 0%
where the time goes in v1:
time: 2780 us; the launch traced here: 2750 us
  blocking collectives  988 us (36%)
  local copies, waits for them, and re-layouts  882 us (32%)
  other arithmetic  680 us (24%)
  matrix products  96.7 us (3%)
  waiting for transfers between devices  55.2 us (2%)
  starting transfers between devices  33.9 us (1%)
    unnamed x1, blocking collectives  964 us
    all_gather x1, other arithmetic, per_device(): ffn_full = lax.all_gather(ffn_params, 'fsdp', axis=0, tiled=True)  401 us
    unnamed x304, local copies, waits for them, and re-layouts  333 us
    all_gather x1, other arithmetic, per_device(): cross_full = lax.all_gather(cross_params, 'fsdp', axis=0, tiled=True)  142 us
    reshape x6, local copies, waits for them, and re-layouts, regroup(): return flat_vec.reshape(groups, replicas, -1).transpose(1, 0, 2).reshape(-1)  133 us
    all_gather x1, other arithmetic, per_device(): lax.all_gather(self_params, 'fsdp', axis=0, tiled=True)  77.7 us
    slice x8, local copies, waits for them, and re-layouts, split_flat(): pieces.append(flat_vec[offset:offset + amount].reshape(layout))  56 us
  transfers between devices with their start and end apart: 19, of which 11 were waited for; matrix products, arithmetic and copies ran while one was open for 17% of the time, Pallas kernels for 0%

profile of v1, /device:TPU:0, one launch (start us, length us, event | category | flops | bytes accessed | tf_op | source)
XLA Modules:
  0.0 2751.9 jit_solution(10041021026785746451)
XLA Ops:
  54.0 14.2 reshape.511
  72.9 10.6 collective-permute-done.7
  245.1 77.7 %reduce.13 = bf16[16,147712]{1,0:T(8,128)(2,1)} reduce(bf16[16,1,147712]{2,1,0:T(2,128)(2,1)} %all-gather.15.cloned.1.call-done, bf16[]{:T(256)} %constant.189), dimensions={1}, to_apply=%all-gather.2.reduce_sub_computation | reduce | bytes 9453570 | tf_op jit(solution)/shard_map/all_gather | solution.py:269
  322.9 10.2 reshape.514
  348.9 141.7 %reduce.11 = bf16[16,209152]{1,0:T(8,128)(2,1)} reduce(bf16[16,1,209152]{2,1,0:T(2,128)(2,1)} %all-gather.11.cloned.1.call-done, bf16[]{:T(256)} %constant.189), dimensions={1}, to_apply=%all-gather.reduce_sub_computation | reduce | bytes 13385730 | tf_op jit(solution)/shard_map/all_gather | solution.py:195
  490.6 13.7 reshape.510
  559.4 400.6 %reduce.12 = bf16[16,590592]{1,0:T(8,128)(2,1)} reduce(bf16[16,1,590592]{2,1,0:T(2,128)(2,1)} %all-gather.13.cloned.1.call-done, bf16[]{:T(256)} %constant.189), dimensions={1}, to_apply=%all-gather.1.reduce_sub_computation | reduce | bytes 37797888 | tf_op jit(solution)/shard_map/all_gather | solution.py:211
  960.0 43.1 %reshape.512 = bf16[9449472]{0:T(1024)(128)(2,1)} reshape(bf16[16,590592]{1,0:T(8,128)(2,1)} %reduce.12) | data formatting | bytes 37797888
  1003.1 14.0 fusion.72
  1019.8 8.2 slice.176
  1028.1 9.3 slice.179
  1050.5 9.2 slice.187
  1059.8 8.2 reshape.478
  1179.8 8.7 pad.12
  1188.5 10.3 reshape.495
  1282.6 10.0 pad.13
  1292.6 13.4 reshape.501
  1306.0 10.5 copy.147
  1316.5 10.0 reshape.502
  1336.2 10.8 reshape.504
  1354.1 10.7 reshape.506
  1365.4 8.3 constant_dynamic-update-slice_fusion.6
  1377.7 80.5 %dynamic-update-slice.6 = f32[9447936]{0:T(1024)} dynamic-update-slice(f32[9447936]{0:T(1024)} %constant_dynamic-update-slice_fusion.25, f32[2359296]{0:T(1024)} %bitcast.182, s32[]{} %constant.201) | dynamic-update-slice | bytes 18874372
  1459.5 80.5 %dynamic-update-slice.8 = f32[9447936]{0:T(1024)} dynamic-update-slice(f32[9447936]{0:T(1024)} %constant_dynamic-update-slice_fusion.24, f32[2359296]{0:T(1024)} %reshape.506, s32[]{} %constant.203) | dynamic-update-slice | bytes 18874372
  1543.9 27.1 pad.14
  1570.9 59.6 %reshape.507 = f32[16,2,295296]{2,1,0:T(2,128)} reshape(f32[9449472]{0:T(1024)} %pad.14) | data formatting | bytes 75595776 | tf_op jit(solution)/shard_map/reshape | solution.py:48
  1630.5 29.9 %copy.148 = f32[2,16,295296]{2,1,0:T(8,128)} copy(f32[2,16,295296]{2,0,1:T(2,128)} %bitcast.175) | data formatting | bytes 75595776 | tf_op jit(solution)/shard_map/transpose | solution.py:48
  1660.4 31.6 %reshape.508 = f32[9449472]{0:T(1024)} reshape(f32[2,16,295296]{2,1,0:T(8,128)} %copy.148) | data formatting | bytes 75595776 | tf_op jit(solution)/shard_map/reshape | solution.py:48
  1692.0 963.5 %all-reduce.8 = (bf16[2363392]{0:T(1024)(128)(2,1)}, bf16[3346432]{0:T(1024)(128)(2,1)}, bf16[9449472]{0:T(1024)(128)(2,1)}) all-reduce(f32[2363392]{0:T(1024)} %reshape.496, f32[3346432]{0:T(1024)} %reshape.502, f32[9449472]{0:T(1024)} %reshape.508), channel_id=2, replica_groups=mesh['dp'=2,'fsdp'=16] {'dp','fsdp'}, use_global_device_ids=true, to_apply=%region_28.29.clone | all-reduce | flops 15159296 | bytes 90955776
  2656.7 9.1 all-gather.3
  2678.3 15.3 all-gather.4
  2714.9 26.9 convert_reduce_fusion
  (534 shorter events, 558.7 us)
Async XLA Ops:
  7.2 237.9 %all-gather.15.cloned.1.call-start = ((), (), s32[]{:S(2)}) async-start(), calls=%async_computation.2 | async-start | bytes 10044416 | tf_op jit(solution)/shard_map/all_gather | solution.py:269
  11.7 61.0 %copy-start.124 = (s32[2]{0:T(128)S(1)}, s32[2]{0:T(128)}, u32[]{:S(2)}) copy-start(s32[2]{0:T(128)} %param.8) | copy-start | bytes 28
  11.7 61.1 %copy-start.28 = (bf16[2,64,768]{2,1,0:T(8,128)(2,1)S(1)}, bf16[2,64,768]{2,1,0:T(8,128)(2,1)}, u32[]{:S(2)}) copy-start(bf16[2,64,768]{2,1,0:T(8,128)(2,1)} %param.10) | copy-start | bytes 589828
  11.7 337.2 %all-gather.11.cloned.1.call-start = ((), (), s32[]{:S(2)}) async-start(), calls=%async_computation | async-start | bytes 14222336 | tf_op jit(solution)/shard_map/all_gather | solution.py:195
  17.4 98.9 %copy-start.50 = (bf16[2,257,1408]{2,0,1:T(2,128)(2,1)S(1)}, bf16[2,257,1408]{2,0,1:T(2,128)(2,1)}, u32[]{:S(2)}) copy-start(bf16[2,257,1408]{2,0,1:T(2,128)(2,1)} %param.9) | copy-start | bytes 4342276
  17.4 542.0 %all-gather.13.cloned.1.call-start = ((), (), s32[]{:S(2)}) async-start(), calls=%async_computation.1 | async-start | bytes 40160256 | tf_op jit(solution)/shard_map/all_gather | solution.py:211
  17.5 10.3 collective-permute-start
  18.0 15.7 collective-permute-start.1
  27.8 15.2 collective-permute-start.2
  33.6 82.7 %copy-start.70 = (bf16[147712]{0:T(1024)(128)(2,1)}, bf16[147712]{0:T(1024)(128)(2,1)S(1)}, u32[]{:S(2)}) copy-start(bf16[147712]{0:T(1024)(128)(2,1)S(1)} %collective-permute-done.1) | copy-start | bytes 886276
  33.6 15.1 collective-permute-start.3
  43.0 10.9 collective-permute-start.4
  48.7 19.5 collective-permute-start.5
  54.0 18.8 collective-permute-start.6
  68.2 2646.7 %all-gather.17.cloned.1.call-start = ((), (), s32[]{:S(2)}) async-start(), calls=%async_computation.3 | async-start | bytes 3543552 | tf_op jit(solution)/shard_map/all_gather | solution.py:320
  68.2 15.3 collective-permute-start.7
  72.7 15.5 collective-permute-start.8
  83.5 11.9 collective-permute-start.9
  88.2 11.9 collective-permute-start.10
  95.4 13.3 collective-permute-start.11
  100.1 14.9 collective-permute-start.12
  108.7 94.6 %collective-permute-start.13 = (bf16[147712]{0:T(1024)(128)(2,1)}, bf16[147712]{0:T(1024)(128)(2,1)}, u32[]{:S(2)}, u32[]{:S(2)}) collective-permute-start(bf16[147712]{0:T(1024)(128)(2,1)} %collective-permute-done.11), channel_id=1, source_target_pairs={{0,15},{1,0},{2,1},{3,2},{4,3},{5,4},{6,5},{7,6},{8,7},{9,8},{10,9... | collective-permute-start | bytes 886280 | tf_op jit(solution)/shard_map/ppermute | solution.py:166
  115.0 94.2 %collective-permute-start.14 = (bf16[147712]{0:T(1024)(128)(2,1)}, bf16[147712]{0:T(1024)(128)(2,1)}, u32[]{:S(2)}, u32[]{:S(2)}) collective-permute-start(bf16[147712]{0:T(1024)(128)(2,1)} %collective-permute-done.12), channel_id=1, source_target_pairs={{0,1},{1,2},{2,3},{3,4},{4,5},{5,6},{6,7},{7,8},{8,9},{9,10},{10,1... | collective-permute-start | bytes 886280 | tf_op jit(solution)/shard_map/ppermute | solution.py:163
  118.0 56.0 %copy-start.77 = (bf16[147712]{0:T(1024)(128)(2,1)S(1)}, bf16[147712]{0:T(1024)(128)(2,1)}, u32[]{:S(2)}) copy-start(bf16[147712]{0:T(1024)(128)(2,1)} %copy-done.76) | copy-start | bytes 886276
  120.5 59.3 %copy-start.79 = (bf16[147712]{0:T(1024)(128)(2,1)S(1)}, bf16[147712]{0:T(1024)(128)(2,1)}, u32[]{:S(2)}) copy-start(bf16[147712]{0:T(1024)(128)(2,1)} %copy-done.78) | copy-start | bytes 886276
  120.5 65.1 %copy-start.81 = (bf16[147712]{0:T(1024)(128)(2,1)S(1)}, bf16[147712]{0:T(1024)(128)(2,1)}, u32[]{:S(2)}) copy-start(bf16[147712]{0:T(1024)(128)(2,1)} %copy-done.80) | copy-start | bytes 886276
  239.2 83.7 %copy-start.30 = (bf16[128,768]{0,1:T(8,128)(2,1)}, bf16[128,768]{0,1:T(8,128)(2,1)S(1)}, u32[]{:S(2)}) copy-start(bf16[128,768]{0,1:T(8,128)(2,1)S(1)} %convert_element_type.316) | copy-start | bytes 589828
  243.7 79.2 %copy-start.36 = (f32[2,32,768]{2,1,0:T(8,128)}, f32[2,32,768]{2,1,0:T(8,128)S(1)}, u32[]{:S(2)}) copy-start(f32[2,32,768]{2,1,0:T(8,128)S(1)} %get-tuple-element.76) | copy-start | bytes 589828
  1377.7 80.5 %copy-start.114 = (f32[3072]{0:T(1024)S(1)}, f32[3072]{0:T(1024)}, u32[]{:S(2)}) copy-start(f32[3072]{0:T(1024)} %get-tuple-element.21) | copy-start | bytes 36868
  1459.5 80.5 %copy-start.105 = (f32[768]{0:T(1024)S(1)}, f32[768]{0:T(1024)}, u32[]{:S(2)}) copy-start(f32[768]{0:T(1024)} %get-tuple-element.19) | copy-start | bytes 9220
  1459.5 81.8 %copy-start.104 = (f32[768]{0:T(1024)S(1)}, f32[768]{0:T(1024)}, u32[]{:S(2)}) copy-start(f32[768]{0:T(1024)} %get-tuple-element.7) | copy-start | bytes 9220
  1459.5 83.1 %copy-start.100 = (f32[768]{0:T(1024)S(1)}, f32[768]{0:T(1024)}, u32[]{:S(2)}) copy-start(f32[768]{0:T(1024)} %get-tuple-element.13) | copy-start | bytes 9220
  (118 other events, 864.5 us)
Sparse Core Ops, SparseCore 0:
  11.8 106.7 all-gather.14
  121.5 107.5 all-gather.10
  231.3 186.1 all-gather.12
  2678.4 36.3 all-gather.16
